TPU v7x, 32 devices: a whole 2x2x4 slice. The times are simulated.
32 devices in a mesh: dp: 8 (over z, core), filter: 4 (over y, x).
Axes of the slice: x: 2, y: 2, z: 4, core: 2. Of those that a mesh axis runs over, the one named last changes fastest.
Arguments:
- patches: bfloat16 [256, 24, 2048], P('filter', 'dp'), may hold values from -6 to 6
- cotangent: bfloat16 [256, 24, 2048], P('filter', 'dp'), may hold values from -6 to 6
- first_weight: bfloat16 [27, 256, 256], P(None, 'filter'), may hold values from -0.078125 to 0.078125
- second_weight: bfloat16 [27, 256, 256], P(None, 'filter'), may hold values from -0.078125 to 0.078125
- counts: int32 [8], P('dp'), may hold values from 0 to 3, as said below
Outputs:
- output_maps: float32 [256, 24, 2048], P('filter', 'dp')
- input_grad: float32 [256, 24, 2048], P('filter', 'dp')
- first_grad: float32 [27, 256, 256], P(None, 'filter')
- second_grad: float32 [27, 256, 256], P(None, 'filter')
Inputs may be any that keep to these rules, and one draw needn't show every extreme that they name: The counts of all groups sum to 8; one group holds exactly 3 live patches. Live patches of a group occupy its first slots.
All inputs are finite; a program needn't handle non-finite values.
Results may differ from a plain program's by a relative error of at most 0.0029.
Values may be sent and summed in bfloat16 or wider, within the bound.
A program may use at most 192 MiB of HBM per device.

v0:
```python
import jax
import jax.numpy as jnp
from jax import lax
from jax.sharding import PartitionSpec as P

PX = 8
PY = 16
PZ = 16
CAP = 3
CELLS = 2048


stencil_taps = [(ox, oy, oz) for ox in (-1, 0, 1) for oy in (-1, 0, 1) for oz in (-1, 0, 1)]


def shift_cells(value, ox, oy, oz):
    span = PY * PZ + PZ + 1
    step = ox * PY * PZ + oy * PZ + oz
    padded = jnp.pad(value, [(0, 0)] * (value.ndim - 1) + [(span, span)])
    moved = lax.slice_in_dim(padded, span + step, span + step + CELLS, axis=value.ndim - 1)
    cell = jnp.arange(CELLS, dtype=jnp.int32)
    pos_x = cell // (PY * PZ) + ox
    pos_y = cell // PZ % PY + oy
    pos_z = cell % PZ + oz
    inside = (pos_x >= 0) & (pos_x < PX) & (pos_y >= 0) & (pos_y < PY) & (pos_z >= 0) & (pos_z < PZ)
    return jnp.where(inside, moved, jnp.zeros_like(moved))


def shifted_stack(value):
    return jnp.stack([shift_cells(value, -ox, -oy, -oz) for ox, oy, oz in stencil_taps])


def forward_conv(inputs, weight):
    proj = jnp.einsum("toi,isc->tosc", weight, inputs, preferred_element_type=jnp.float32)
    total = jnp.zeros(proj.shape[1:], jnp.float32)
    for t, (ox, oy, oz) in enumerate(stencil_taps):
        total = total + shift_cells(proj[t], ox, oy, oz)
    return total


def weight_conv(grads, inputs):
    stack = shifted_stack(grads)
    return jnp.einsum("tosc,isc->toi", stack, inputs, preferred_element_type=jnp.float32)


def backward_conv(grads, weight):
    stack = shifted_stack(grads)
    return lax.psum_scatter(
        jnp.einsum("toi,tosc->isc", weight, stack, preferred_element_type=jnp.float32),
        "filter",
        scatter_dimension=0,
        tiled=True,
    )


def layer_pair(inputs, masked, first_weight, second_weight):
    full_inputs = lax.all_gather(inputs, "filter", axis=0, tiled=True)
    first = forward_conv(full_inputs, first_weight)
    hidden = jax.nn.silu(first).astype(jnp.bfloat16)
    full_hidden = lax.all_gather(hidden, "filter", axis=0, tiled=True)
    result = forward_conv(full_hidden, second_weight)
    hidden_grad = backward_conv(masked, second_weight)
    second_part = weight_conv(masked, full_hidden)
    sigma = jax.nn.sigmoid(first)
    delta = (hidden_grad * sigma * (1.0 + first * (1.0 - sigma))).astype(jnp.bfloat16)
    in_grad = backward_conv(delta, first_weight)
    first_part = weight_conv(delta, full_inputs)
    return (result, in_grad, first_part, second_part)


def shards(patches, cotangent, first_weight, second_weight, counts):
    live = (jnp.arange(CAP, dtype=jnp.int32) < counts[0]).astype(jnp.bfloat16)
    masked = cotangent * live[None, :, None]
    result, in_grad, first_part, second_part = layer_pair(
        patches, masked, first_weight, second_weight
    )
    output_maps = result * live[None, :, None].astype(jnp.float32)
    first_sum, second_sum = lax.psum((first_part, second_part), "dp")
    scale = 1.0 / jnp.sqrt(jnp.float32(lax.axis_size("dp") * CELLS))
    return (output_maps, in_grad, first_sum * scale, second_sum * scale)


def solution(mesh):
    placed = (
        P("filter", "dp", None),
        P("filter", "dp", None),
        P(None, "filter", None),
        P(None, "filter", None),
        P("dp"),
    )
    return jax.shard_map(
        shards,
        mesh=mesh,
        in_specs=placed,
        out_specs=(
            P("filter", "dp", None),
            P("filter", "dp", None),
            P(None, "filter", None),
            P(None, "filter", None),
        ),
        check_vma=False,
    )
```

profile of v0, /device:TPU:0, one launch (start us, length us, event | category | flops | bytes accessed | tf_op | source)
XLA Modules:
  0.0 493.0 jit_solution(11752355239427686231)
XLA Ops:
  8.8 1.3 broadcast_multiply_fusion.2
  19.5 7.4 %copy-done.12 = bf16[27,64,3,2048]{3,1,2,0:T(8,128)(2,1)} copy-done((bf16[27,64,3,2048]{3,1,2,0:T(8,128)(2,1)}, bf16[27,64,3,2048]{3,1,2,0:T(8,128)(2,1)S(1)}, u32[]{:S(2)}) %copy-start.12) | copy-done | bytes 21233688
  26.9 9.6 %convolution_bitcast_fusion.1 = f32[256,3,2048]{2,0,1:T(8,128)} fusion(bf16[27,64,3,2048]{3,1,2,0:T(8,128)(2,1)S(1)} %fusion.201, bf16[27,64,256]{2,1,0:T(8,128)(2,1)S(1)} %copy-done.10), kind=kOutput, calls=%fused_computation.1 | convolution fusion | flops 5435817984 | bytes 28409856 | tf_op jit(solution)/shard_map/toi,tosc->isc/dot_general | solution.py:49
  39.0 17.6 %all-gather.3.cloned.1.call-done = bf16[256,3,2048]{2,0,1:T(8,128)(2,1)} async-done(((bf16[64,3,2048]{2,0,1:T(8,128)(2,1)}), bf16[256,3,2048]{2,0,1:T(8,128)(2,1)}) %all-gather.3.cloned.1.call-update) | async-done | bytes 3145744 | tf_op jit(solution)/shard_map/all_gather | solution.py:57
  56.6 19.7 %fusion.5 = f32[27,64,3,2048]{3,1,2,0:T(8,128)} fusion(bf16[256,3,2048]{2,0,1:T(8,128)(2,1)} %all-gather.3.cloned.1.call-done, bf16[27,64,256]{2,1,0:T(8,128)(2,1)S(1)} %copy-done), kind=kOutput, calls=%fused_computation.8 | convolution fusion | flops 5435817984 | bytes 46497792 | tf_op jit(solution)/shard_map/toi,isc->tosc/dot_general | solution.py:34
  76.2 8.5 %slice_bitcast_fusion.52 = (f32[64,3,2048]{2,0,1:T(8,128)S(1)}, f32[64,3,2048]{2,0,1:T(8,128)}, f32[64,3,2048]{2,0,1:T(8,128)}, f32[64,3,2048]{2,0,1:T(8,128)}, ...) fusion(f32[27,64,3,2048]{3,1,2,0:T(8,128)} %fusion.5), kind=kLoop, calls=%fused_computation.221 | loop fusion | bytes 22020096 | tf_op jit(solution)/shard_map/squeeze | solution.py:37
  84.7 18.9 %slice_bitcast_fusion.53 = (f32[64,3,2048]{2,0,1:T(8,128)}, f32[64,3,2048]{2,0,1:T(8,128)}, f32[64,3,2048]{2,0,1:T(8,128)}, f32[64,3,2048]{2,0,1:T(8,128)}, f32[...) fusion(f32[27,64,3,2048]{3,1,2,0:T(8,128)} %fusion.5), kind=kLoop, calls=%fused_computation.222 | loop fusion | bytes 59768832 | tf_op jit(solution)/shard_map/squeeze | solution.py:37
  103.6 26.2 %reduce-scatter.2.cloned.1.call-done = f32[64,3,2048]{2,0,1:T(8,128)} async-done(((f32[256,3,2048]{2,0,1:T(8,128)}), f32[64,3,2048]{2,0,1:T(8,128)}) %reduce-scatter.2.cloned.1.call-update) | async-done | bytes 1572880 | tf_op jit(solution)/shard_map/reduce_scatter | solution.py:48
  129.8 16.9 %multiply_convert_fusion = (bf16[64,3,2048]{2,0,1:T(8,128)(2,1)S(1)}, f32[64,3,2048]{2,0,1:T(8,128)S(1)}) fusion(f32[64,3,2048]{2,0,1:T(8,128)} %reduce-scatter.2.cloned.1.call-done, f32[64,3,2048]{2,0,1:T(8,128)} %get-tuple-element.43, pred[2048]{0:T(1024)(128)(4,1)S(1)} %get-tuple-element.68, f32[64,3,2048]{2,0,1:T(8,128)} %get-tuple-element.44, ...), kind=kLoop, calls=%fused_computation.223 | loop fusion | flops 24379392 | bytes 46454784 | tf_op jit(solution)/shard_map/convert_element_type | solution.py:65
  146.8 1.2 fusion.204
  148.0 1.2 fusion.207
  150.4 1.2 fusion.213
  152.6 1.2 fusion.219
  153.8 1.3 fusion.222
  155.1 1.2 fusion.225
  156.3 1.2 fusion.228
  157.5 1.3 fusion.231
  158.8 1.3 fusion.234
  160.1 1.2 fusion.237
  161.4 1.3 fusion.240
  163.7 1.3 fusion.243
  164.9 1.3 fusion.246
  166.2 1.3 fusion.249
  167.5 1.3 fusion.252
  168.8 1.2 fusion.255
  170.0 1.3 fusion.258
  171.3 1.2 fusion.261
  172.5 1.3 multiply_convert_fusion.1
  173.9 1.2 fusion.264
  176.2 1.2 fusion.270
  177.4 1.2 fusion.273
  178.6 1.2 fusion.276
  179.8 1.2 fusion.279
  181.0 12.6 %convolution_bitcast_fusion.2 = f32[256,3,2048]{0,2,1:T(8,128)} fusion(bf16[27,64,3,2048]{3,1,2,0:T(8,128)(2,1)} %fusion.279, bf16[27,64,256]{2,1,0:T(8,128)(2,1)S(1)} %copy-done), kind=kOutput, calls=%fused_computation.2 | convolution fusion | flops 5435817984 | bytes 28409856 | tf_op jit(solution)/shard_map/toi,tosc->isc/dot_general | solution.py:49
  193.6 9.7 %copy.18 = f32[256,3,2048]{2,1,0:T(4,128)} copy(f32[256,3,2048]{0,2,1:T(8,128)} %convolution_bitcast_fusion.2) | data formatting | bytes 12582912 | tf_op jit(solution)/shard_map/toi,tosc->isc/dot_general | solution.py:49
  203.4 12.0 %fusion.114 = f32[27,64,256]{2,1,0:T(8,128)} fusion(bf16[27,64,3,2048]{3,1,2,0:T(8,128)(2,1)} %fusion.279, bf16[256,3,2048]{2,0,1:T(8,128)(2,1)} %all-gather.3.cloned.1.call-done), kind=kOutput, calls=%fused_computation.226 | convolution fusion | flops 5435817984 | bytes 26148864 | tf_op jit(solution)/shard_map/tosc,isc->toi/dot_general | solution.py:43
  215.5 2.5 all-gather.5.cloned.1.call-done
  218.0 19.6 %convolution_bitcast_fusion = f32[27,64,3,2048]{3,1,2,0:T(8,128)} fusion(bf16[256,3,2048]{2,0,1:T(8,128)(2,1)} %all-gather.5.cloned.1.call-done, bf16[27,64,256]{2,1,0:T(8,128)(2,1)S(1)} %copy-done.11), kind=kOutput, calls=%fused_computation | convolution fusion | flops 5435817984 | bytes 46497792 | tf_op jit(solution)/shard_map/toi,isc->tosc/dot_general | solution.py:34
  237.6 20.0 %slice_bitcast_fusion.26 = (f32[64,3,2048]{2,0,1:T(8,128)S(1)}, f32[64,3,2048]{2,0,1:T(8,128)}, f32[64,3,2048]{2,0,1:T(8,128)}, f32[64,3,2048]{2,0,1:T(8,128)}, ...) fusion(f32[27,64,3,2048]{3,1,2,0:T(8,128)} %convolution_bitcast, ...), kind=kLoop, calls=%fused_computation.194 | loop fusion | bytes 59768832 | tf_op jit(solution)/shard_map/squeeze | solution.py:37
  257.6 12.3 %fusion.117 = f32[27,64,256]{2,1,0:T(8,128)} fusion(bf16[27,64,3,2048]{3,1,2,0:T(8,128)(2,1)} %copy-done.12, bf16[256,3,2048]{2,0,1:T(8,128)(2,1)} %all-gather.5.cloned.1.call-done), kind=kOutput, calls=%fused_computation.227 | convolution fusion | flops 5435817984 | bytes 26148864 | tf_op jit(solution)/shard_map/tosc,isc->toi/dot_general | solution.py:43
  270.0 9.8 %slice_bitcast_fusion.25 = (f32[64,3,2048]{2,0,1:T(8,128)}, f32[64,3,2048]{2,0,1:T(8,128)}, f32[64,3,2048]{2,0,1:T(8,128)}, f32[64,3,2048]{2,0,1:T(8,128)}, f32[...) fusion(f32[27,64,3,2048]{3,1,2,0:T(8,128)} %convolution_bitcast_fusion), kind=kLoop, calls=%fused_computation.193 | loop fusion | bytes 22020096 | tf_op jit(solution)/shard_map/squeeze | solution.py:37
  280.4 16.4 %fusion.109 = f32[64,3,2048]{2,0,1:T(8,128)} fusion(f32[64,3,2048]{2,0,1:T(8,128)S(1)} %copy-done.4, f32[64,3,2048]{2,0,1:T(8,128)S(1)} %copy-done.3, f32[64,3,2048]{2,0,1:T(8,128)S(1)} %copy-done.2, f32[64,3,2048]{2,0,1:T(8,128)S(1)} %copy-done.5, f32[64,3,2048]{2,0,1:T(8,128)S(1)} %copy-done.6, f32[64,3,2048]{2,0,1:T(8,128)S(1)} %copy-done.7, ...), kind=kLoop, calls=%fused_computation.164 | loop fusion | flops 21233664 | bytes 44095500 | tf_op jit(solution)/shard_map/mul | solution.py:77
  296.8 96.7 %all-reduce.59.cloned.1.call-done = f32[256,3,2048]{2,1,0:T(4,128)} async-done(((f32[256,3,2048]{2,1,0:T(4,128)}), f32[256,3,2048]{2,1,0:T(4,128)}) %all-reduce.59.cloned.1.call-update) | async-done | bytes 6291472
  393.5 2.0 constant_dynamic-slice_fusion
  395.4 2.1 copy.19
  397.5 84.2 %all-reduce.61.cloned.1.call-done = (f32[27,64,256]{2,1,0:T(8,128)}, f32[27,64,256]{2,1,0:T(8,128)}) async-done(((f32[27,64,256]{2,1,0:T(8,128)}, f32[27,64,256]{2,1,0:T(8,128)}), (f32[27,64,256]{2,1,0:T(8,128)}, f32[27,64,256]{2,1,0:T(8,128)})) %all-reduce.61.cloned.1.call-update) | async-done | bytes 3538960 | tf_op jit(solution)/shard_map/psum | solution.py:78
  481.7 3.0 broadcast_multiply_fusion
  484.7 1.3 broadcast_multiply_fusion.1
  (87 shorter events, 17.1 us)
Async XLA Ops:
  7.2 49.4 %copy-start = (bf16[27,64,256]{2,1,0:T(8,128)(2,1)S(1)}, bf16[27,64,256]{2,1,0:T(8,128)(2,1)}, u32[]{:S(2)}) copy-start(bf16[27,64,256]{2,1,0:T(8,128)(2,1)} %param.7) | copy-start | bytes 2654212
  7.2 49.4 %all-gather.3.cloned.1.call-start = ((), (), s32[]{:S(2)}) async-start(), calls=%async_computation.1 | async-start | bytes 3932160 | tf_op jit(solution)/shard_map/all_gather | solution.py:57
  7.9 121.9 %reduce-scatter.2.cloned.1.call-start = ((), (), s32[]{:S(2)}) async-start(), calls=%async_computation.3 | async-start | bytes 7864320 | tf_op jit(solution)/shard_map/reduce_scatter | solution.py:48
  13.6 1.1 copy-start.8
  18.8 8.1 %copy-start.10 = (bf16[27,64,256]{2,1,0:T(8,128)(2,1)S(1)}, bf16[27,64,256]{2,1,0:T(8,128)(2,1)}, u32[]{:S(2)}) copy-start(bf16[27,64,256]{2,1,0:T(8,128)(2,1)} %param.8) | copy-start | bytes 2654212
  19.5 7.5 %copy-start.12 = (bf16[27,64,3,2048]{3,1,2,0:T(8,128)(2,1)}, bf16[27,64,3,2048]{3,1,2,0:T(8,128)(2,1)S(1)}, u32[]{:S(2)}) copy-start(bf16[27,64,3,2048]{3,1,2,0:T(8,128)(2,1)S(1)} %fusion.201) | copy-start | bytes 63700996
  36.5 0.7 copy-start.14
  36.6 181.4 %all-gather.5.cloned.1.call-start = ((), (), s32[]{:S(2)}) async-start(), calls=%async_computation.2 | async-start | bytes 3932160 | tf_op jit(solution)/shard_map/all_gather | solution.py:60
  173.8 219.7 %all-reduce.59.cloned.1.call-start = ((), (), s32[]{:S(2)}) async-start(), calls=%async_computation.4 | async-start | bytes 16777216
  203.4 14.6 %copy-start.11 = (bf16[27,64,256]{2,1,0:T(8,128)(2,1)S(1)}, bf16[27,64,256]{2,1,0:T(8,128)(2,1)}, u32[]{:S(2)}) copy-start(bf16[27,64,256]{2,1,0:T(8,128)(2,1)} %param.8) | copy-start | bytes 2654212
  203.4 278.4 %all-reduce.61.cloned.1.call-start = ((), (), s32[]{:S(2)}) async-start(), calls=%async_computation.5 | async-start | bytes 7077888 | tf_op jit(solution)/shard_map/psum | solution.py:78
  269.9 9.9 %copy-start.2 = (f32[64,3,2048]{2,0,1:T(8,128)S(1)}, f32[64,3,2048]{2,0,1:T(8,128)}, u32[]{:S(2)}) copy-start(f32[64,3,2048]{2,0,1:T(8,128)} %get-tuple-element.17) | copy-start | bytes 4718596
  269.9 9.9 %copy-start.3 = (f32[64,3,2048]{2,0,1:T(8,128)S(1)}, f32[64,3,2048]{2,0,1:T(8,128)}, u32[]{:S(2)}) copy-start(f32[64,3,2048]{2,0,1:T(8,128)} %get-tuple-element.18) | copy-start | bytes 4718596
  269.9 9.9 %copy-start.4 = (f32[64,3,2048]{2,0,1:T(8,128)S(1)}, f32[64,3,2048]{2,0,1:T(8,128)}, u32[]{:S(2)}) copy-start(f32[64,3,2048]{2,0,1:T(8,128)} %get-tuple-element.19) | copy-start | bytes 4718596
  269.9 9.9 %copy-start.5 = (f32[64,3,2048]{2,0,1:T(8,128)S(1)}, f32[64,3,2048]{2,0,1:T(8,128)}, u32[]{:S(2)}) copy-start(f32[64,3,2048]{2,0,1:T(8,128)} %get-tuple-element.20) | copy-start | bytes 4718596
  269.9 9.9 %copy-start.6 = (f32[64,3,2048]{2,0,1:T(8,128)S(1)}, f32[64,3,2048]{2,0,1:T(8,128)}, u32[]{:S(2)}) copy-start(f32[64,3,2048]{2,0,1:T(8,128)} %get-tuple-element.21) | copy-start | bytes 4718596
  269.9 10.5 %copy-start.7 = (f32[64,3,2048]{2,0,1:T(8,128)S(1)}, f32[64,3,2048]{2,0,1:T(8,128)}, u32[]{:S(2)}) copy-start(f32[64,3,2048]{2,0,1:T(8,128)} %get-tuple-element.22) | copy-start | bytes 4718596
  270.0 10.5 %copy-start.13 = (f32[3]{0:T(128)S(1)}, f32[3]{0:T(128)}, u32[]{:S(2)}) copy-start(f32[3]{0:T(128)} %fusion.309) | copy-start | bytes 40
  481.7 3.0 copy-start.9
  484.7 1.5 copy-start.1
Sparse Core Ops, SparseCore 0:
  9.9 46.6 all-gather.2
  59.6 70.2 reduce-scatter.1
  174.0 43.9 all-gather.4
  221.3 172.0 all-reduce.58
  396.5 85.2 all-reduce.60
where the time goes:
time: 500 us; the launch traced here: 493 us
  waiting for transfers between devices  228 us (46%)
  matrix products  85.7 us (17%)
  other arithmetic  82.6 us (17%)
  local copies, waits for them, and re-layouts  80.7 us (16%)
  between operations  15.8 us (3%)
    unnamed x6, waiting for transfers between devices  97.5 us
    psum x1, waiting for transfers between devices, shards(): first_sum, second_sum = lax.psum((first_part, second_part), 'dp')  84.2 us
    squeeze x4, local copies, waits for them, and re-layouts, forward_conv(): total = total + shift_cells(proj[t], ox, oy, oz)  57.2 us
    unnamed x52, other arithmetic  40.1 us
    dot_general x2, matrix products, forward_conv(): jnp.einsum('toi,isc->tosc', weight, inputs, preferred_element_type=jnp.fl...  39.3 us
    reduce_scatter x1, waiting for transfers between devices, backward_conv(): lax.psum_scatter(jnp.einsum('toi,tosc->isc', weight, stack, preferred_ele...  26.2 us
    dot_general x2, matrix products, weight_conv(): jnp.einsum('tosc,isc->toi', stack, inputs, preferred_element_type=jnp.flo...  24.3 us
    dot_general x2, matrix products, backward_conv(): jnp.einsum('toi,tosc->isc', weight, stack, preferred_element_type=jnp.flo...  22.2 us
  transfers between devices with their start and end apart: 5, of which 5 were waited for; matrix products, arithmetic and copies ran while one was open for 39% of the time, Pallas kernels for 0%

commit v1 on v0

v1 whole, which is shorter than its diff:
```python
import functools
import math

import jax
import jax.numpy as jnp
from jax import lax
from jax.experimental import pallas as pl
from jax.experimental.pallas import tpu as pltpu
from jax.sharding import PartitionSpec as P

CAP = 3
CELLS = 2048
PLANE = 256
PLANES = 8
SIDE = 16
MESH = pl.DeviceIdType.MESH
F32 = jnp.float32
BF16 = jnp.bfloat16

PAIRS = [(oy, oz) for oy in (-1, 0, 1) for oz in (-1, 0, 1)]


def inside(oy, oz):
    cell = lax.broadcasted_iota(jnp.int32, (1, PLANE), 1)
    y = cell // SIDE + oy
    z = cell % SIDE + oz
    return (y >= 0) & (y < SIDE) & (z >= 0) & (z < SIDE)


def moved(value, oy, oz):
    step = oy * SIDE + oz
    if step == 0:
        return value
    rolled = pltpu.roll(value, (-step) % PLANE, 1)
    return jnp.where(inside(oy, oz), rolled, jnp.zeros_like(rolled))


def remote(src, dst, send, recv, target):
    return pltpu.make_async_remote_copy(
        src_ref=src, dst_ref=dst, send_sem=send, recv_sem=recv, device_id=target, device_id_type=MESH
    )


def build_stack(c, value, stack):
    zero = jnp.zeros((9 * c, PLANE), BF16)
    stack[0 : 9 * c, PLANES * PLANE : (PLANES + 1) * PLANE] = zero
    stack[18 * c : 27 * c, PLANE : 2 * PLANE] = zero

    def plane(p, _):
        part = value[:, pl.ds(pl.multiple_of(p * PLANE, PLANE), PLANE)].astype(F32)
        for j, (oy, oz) in enumerate(PAIRS):
            shifted = moved(part, -oy, -oz).astype(BF16)
            for ox in (-1, 0, 1):
                row = (9 * (ox + 1) + j) * c
                at = pl.multiple_of((p + ox + 1) * PLANE, PLANE)
                stack[row : row + c, pl.ds(at, PLANE)] = shifted
        return 0

    lax.fori_loop(0, PLANES, plane, 0)


def forward(c, value, weight, proj, finish):
    rows = 27 * c
    proj[0, 18 * c : rows, :] = jnp.zeros((9 * c, PLANE), F32)
    proj[0, 0 : 9 * c, :] = jnp.zeros((9 * c, PLANE), F32)
    proj[PLANES + 1, 18 * c : rows, :] = jnp.zeros((9 * c, PLANE), F32)

    def multiply(p, _):
        part = value[:, pl.ds(pl.multiple_of(p * PLANE, PLANE), PLANE)]
        proj[p + 1] = jnp.dot(weight[...], part, preferred_element_type=F32)
        return 0

    lax.fori_loop(0, PLANES, multiply, 0)

    def combine(q, _):
        total = jnp.zeros((c, PLANE), F32)
        for j, (oy, oz) in enumerate(PAIRS):
            terms = [
                proj[q + 1 + ox, (9 * (ox + 1) + j) * c : (9 * (ox + 1) + j + 1) * c, :] for ox in (-1, 0, 1)
            ]
            total = total + moved(terms[0] + terms[1] + terms[2], oy, oz)
        finish(q, total)
        return 0

    lax.fori_loop(0, PLANES, combine, 0)


def backward(weight_t, stack, out):
    def plane(q, _):
        part = stack[:, pl.ds(pl.multiple_of((q + 1) * PLANE, PLANE), PLANE)]
        value = jnp.dot(weight_t[...], part, preferred_element_type=F32)
        out[:, pl.ds(pl.multiple_of(q * PLANE, PLANE), PLANE)] = value.astype(out.dtype)
        return 0

    lax.fori_loop(0, PLANES, plane, 0)


def weight_grad(c, stack, value, out):
    for part in range(3):
        rows = pl.ds(part * 9 * c, 9 * c)
        out[rows, :] = lax.dot_general(
            stack[rows, PLANE : (PLANES + 1) * PLANE],
            value[...],
            (((1,), (1,)), ((), ())),
            preferred_element_type=F32,
        )
    rest = out.shape[0] - 27 * c
    if rest:
        out[27 * c :, :] = jnp.zeros((rest, out.shape[1]), F32)


def kernel(
    nf, nd, c, scale,
    x, u, w1, w2, w1t, w2t,
    out, igrad, g1, g2,
    xg, hg, stack, proj, hpart, hrecv, first, ipart, irecv, acc1, acc2, half1, half2, snd1, snd2, rcv1, rcv2,
    fs, fr, cs, cr, zs, zr,
):
    f = lax.axis_index("filter")
    d = lax.axis_index("dp")
    nz = nd // 2
    core = lax.rem(d, 2)
    z = d // 2
    mate = d + 1 - 2 * core

    def fpeer(k):
        return lax.rem(f + k, nf)

    def ffrom(k):
        return lax.rem(f + nf - k, nf)

    def zpeer(k):
        return lax.rem(z + k, nz)

    def zfrom(k):
        return lax.rem(z + nz - k, nz)

    barrier = pltpu.get_barrier_semaphore()
    for k in range(1, nf):
        pl.semaphore_signal(barrier, inc=1, device_id={"filter": fpeer(k)}, device_id_type=MESH)
    for k in range(1, nz):
        pl.semaphore_signal(barrier, inc=1, device_id={"dp": zpeer(k) * 2 + core}, device_id_type=MESH)
    pl.semaphore_signal(barrier, inc=1, device_id={"dp": mate}, device_id_type=MESH)
    pl.semaphore_wait(barrier, nf + nz - 1)

    def block(i):
        return pl.ds(pl.multiple_of(i * c, c), c)

    def gather(n, own, full):
        return [
            remote(own, full.at[block(f)], fs.at[n, k], fr.at[n, k], {"filter": fpeer(k)}) for k in range(1, nf)
        ]

    def gathered(n, own, full):
        for k in range(1, nf):
            remote(own, full.at[block(ffrom(k))], fs.at[n, k], fr.at[n, k], {"filter": fpeer(k)}).wait_recv()

    def scatter(n, part, recv):
        return [
            remote(part.at[block(fpeer(k))], recv.at[k], fs.at[n, k], fr.at[n, k], {"filter": fpeer(k)})
            for k in range(1, nf)
        ]

    copies = gather(0, x, xg)
    for copy in copies:
        copy.start()
    xg[block(f), :] = x[...]

    build_stack(c, u, stack)
    backward(w2t, stack, hpart)
    hcopies = scatter(1, hpart, hrecv)
    for copy in hcopies:
        copy.start()

    gathered(0, x, xg)

    def activate(q, total):
        at = pl.ds(pl.multiple_of(q * PLANE, PLANE), PLANE)
        first[:, at] = total
        hg[block(f), at] = (total / (1.0 + jnp.exp(-total))).astype(BF16)

    forward(c, xg, w1, proj, activate)
    own_hidden = hg.at[block(f)]
    gcopies = gather(2, own_hidden, hg)
    for copy in gcopies:
        copy.start()

    gathered(2, own_hidden, hg)
    weight_grad(c, stack, hg, acc2)

    half = acc1.shape[0] // 2
    chunk = half // nz

    def swap(n, acc, recv):
        return remote(
            acc.at[pl.ds(pl.multiple_of((1 - core) * half, half), half)],
            recv, cs.at[n], cr.at[n], {"dp": mate},
        )

    def spread(n, acc, recv, snd, rcv):
        mine = pl.ds(pl.multiple_of(core * half, half), half)
        acc[mine, :] = acc[mine, :] + recv[...]
        started = []
        for k in range(1, nz):
            at = pl.ds(pl.multiple_of(core * half + zpeer(k) * chunk, chunk), chunk)
            snd[k] = acc[at, :].astype(BF16)
            copy = remote(snd.at[k], rcv.at[k], zs.at[n, k], zr.at[n, k], {"dp": zpeer(k) * 2 + core})
            copy.start()
            started.append(copy)
        return started

    def settle(n, acc, started, rcv, out):
        at = pl.ds(pl.multiple_of(core * half + z * chunk, chunk), chunk)
        total = acc[at, :]
        for k in range(1, nz):
            started[k - 1].wait_recv()
            total = total + rcv[k].astype(F32)
        out[at, :] = (total * scale).astype(BF16)
        sent = []
        for k in range(1, nz):
            copy = remote(
                out.at[at], out.at[at], zs.at[n + 2, k], zr.at[n + 2, k], {"dp": zpeer(k) * 2 + core}
            )
            copy.start()
            sent.append(copy)
        return sent

    def share(n, out):
        for k in range(1, nz):
            at = pl.ds(pl.multiple_of(core * half + zfrom(k) * chunk, chunk), chunk)
            remote(
                out.at[at], out.at[at], zs.at[n + 2, k], zr.at[n + 2, k], {"dp": zpeer(k) * 2 + core}
            ).wait_recv()
        mine = pl.ds(pl.multiple_of(core * half, half), half)
        copy = remote(out.at[mine], out.at[mine], cs.at[n + 2], cr.at[n + 2], {"dp": mate})
        copy.start()
        return copy

    def shared(n, out):
        other = pl.ds(pl.multiple_of((1 - core) * half, half), half)
        remote(out.at[other], out.at[other], cs.at[n + 2], cr.at[n + 2], {"dp": mate}).wait_recv()

    swap2 = swap(1, acc2, half2)
    swap2.start()

    for k in range(1, nf):
        hcopies[k - 1].wait_recv()

    def deltas(q, _):
        at = pl.ds(pl.multiple_of(q * PLANE, PLANE), PLANE)
        grad = hpart[block(f), at]
        for k in range(1, nf):
            grad = grad + hrecv[k, :, at]
        a = first[:, at]
        sg = 1.0 / (1.0 + jnp.exp(-a))
        first[:, at] = grad * sg * (1.0 + a * (1.0 - sg))
        return 0

    lax.fori_loop(0, PLANES, deltas, 0)
    build_stack(c, first, stack)

    swap2.wait_recv()
    spread2 = spread(1, acc2, half2, snd2, rcv2)

    weight_grad(c, stack, xg, acc1)
    swap1 = swap(0, acc1, half1)
    swap1.start()
    backward(w1t, stack, ipart)
    icopies = scatter(3, ipart, irecv)
    for copy in icopies:
        copy.start()

    swap1.wait_recv()
    spread1 = spread(0, acc1, half1, snd1, rcv1)
    sent2 = settle(1, acc2, spread2, rcv2, g2)

    def keep(q, total):
        out[:, pl.ds(pl.multiple_of(q * PLANE, PLANE), PLANE)] = total.astype(BF16)

    forward(c, hg, w2, proj, keep)

    sent1 = settle(0, acc1, spread1, rcv1, g1)
    last2 = share(1, g2)

    for k in range(1, nf):
        icopies[k - 1].wait_recv()

    def inputs(q, _):
        at = pl.ds(pl.multiple_of(q * PLANE, PLANE), PLANE)
        grad = ipart[block(f), at].astype(F32)
        for k in range(1, nf):
            grad = grad + irecv[k, :, at].astype(F32)
        igrad[:, at] = grad.astype(BF16)
        return 0

    lax.fori_loop(0, PLANES, inputs, 0)

    last1 = share(0, g1)
    shared(1, g2)
    shared(0, g1)
    for copy in copies + hcopies + gcopies + icopies + [swap1, swap2] + spread1 + spread2:
        copy.wait_send()
    for copy in sent1 + sent2 + [last1, last2]:
        copy.wait_send()


def one_patch(x, u, w1, w2, nf, nd):
    c = x.shape[0]
    rows = 27 * c
    wide = w1.shape[-1]
    padded = -(-rows // (16 * nd)) * 16 * nd
    half = padded // 2
    nz = nd // 2
    chunk = half // nz
    scale = 1.0 / math.sqrt(nd * CELLS)
    w1 = w1.reshape(rows, wide)
    w2 = w2.reshape(rows, wide)
    vmem = pl.BlockSpec(memory_space=pltpu.VMEM)
    shape = jax.ShapeDtypeStruct
    flops = 12 * rows * wide * CELLS
    return pl.pallas_call(
        functools.partial(kernel, nf, nd, c, scale),
        out_shape=(
            shape((c, CELLS), BF16), shape((c, CELLS), BF16), shape((padded, wide), BF16), shape((padded, wide), BF16)
        ),
        in_specs=[vmem] * 6,
        out_specs=(vmem,) * 4,
        scratch_shapes=[
            pltpu.VMEM((wide, CELLS), BF16),
            pltpu.VMEM((wide, CELLS), BF16),
            pltpu.VMEM((rows, CELLS + 2 * PLANE), BF16),
            pltpu.VMEM((PLANES + 2, rows, PLANE), F32),
            pltpu.VMEM((wide, CELLS), F32),
            pltpu.VMEM((nf, c, CELLS), F32),
            pltpu.VMEM((c, CELLS), F32),
            pltpu.VMEM((wide, CELLS), BF16),
            pltpu.VMEM((nf, c, CELLS), BF16),
            pltpu.VMEM((padded, wide), F32),
            pltpu.VMEM((padded, wide), F32),
            pltpu.VMEM((half, wide), F32),
            pltpu.VMEM((half, wide), F32),
            pltpu.VMEM((nz, chunk, wide), BF16),
            pltpu.VMEM((nz, chunk, wide), BF16),
            pltpu.VMEM((nz, chunk, wide), BF16),
            pltpu.VMEM((nz, chunk, wide), BF16),
            pltpu.SemaphoreType.DMA((4, nf)),
            pltpu.SemaphoreType.DMA((4, nf)),
            pltpu.SemaphoreType.DMA((4,)),
            pltpu.SemaphoreType.DMA((4,)),
            pltpu.SemaphoreType.DMA((4, nz)),
            pltpu.SemaphoreType.DMA((4, nz)),
        ],
        compiler_params=pltpu.CompilerParams(
            collective_id=0, has_side_effects=True, vmem_limit_bytes=60 * 1024 * 1024
        ),
        cost_estimate=pl.CostEstimate(flops=flops, bytes_accessed=16 * 1024 * 1024, transcendentals=0),
    )(x, u, w1, w2, w1.T, w2.T)


def shards(nf, nd, patches, cotangent, first_weight, second_weight, counts):
    c = patches.shape[0]
    every = lax.all_gather(counts, "dp", axis=0, tiled=True)
    me = lax.axis_index("dp")
    offset = jnp.sum(jnp.where(jnp.arange(nd) < me, every, 0))
    slot = jnp.arange(CAP, dtype=jnp.int32)
    live = slot < counts[0]
    target = offset + slot
    pairs = jnp.stack([patches, cotangent])
    hit = (target[None, :] == jnp.arange(nd)[:, None]) & live[None, :]
    placed = jnp.zeros((nd, 2, c, CELLS), BF16)
    for j in range(CAP):
        placed = jnp.where(hit[:, j][:, None, None, None], pairs[None, :, :, j], placed)
    got = lax.psum_scatter(placed, "dp", scatter_dimension=0, tiled=False)
    out, igrad, g1, g2 = one_patch(got[0], got[1], first_weight, second_weight, nf, nd)
    back = lax.all_gather(jnp.stack([out, igrad]), "dp", axis=0, tiled=False)
    outs = []
    for n in range(2):
        columns = []
        for j in range(CAP):
            at = jnp.minimum(target[j], nd - 1)
            block = lax.dynamic_index_in_dim(back[:, n], at, 0, keepdims=False).astype(F32)
            columns.append(jnp.where(live[j], block, 0.0))
        outs.append(jnp.stack(columns, axis=1))
    rows = 27 * c
    shape = first_weight.shape
    return (
        outs[0],
        outs[1],
        g1[:rows].astype(F32).reshape(shape),
        g2[:rows].astype(F32).reshape(shape),
    )


def solution(mesh):
    placed = (
        P("filter", "dp", None),
        P("filter", "dp", None),
        P(None, "filter", None),
        P(None, "filter", None),
        P("dp"),
    )
    return jax.shard_map(
        functools.partial(shards, mesh.shape["filter"], mesh.shape["dp"]),
        mesh=mesh,
        in_specs=placed,
        out_specs=(
            P("filter", "dp", None),
            P("filter", "dp", None),
            P(None, "filter", None),
            P(None, "filter", None),
        ),
        check_vma=False,
    )
```

time: 500 us -> 240 us (0.48); the launches traced: 493 us -> 240 us
  waiting for transfers between devices: 228 us -> 87.6 us
  Pallas kernels: 0 us -> 97.9 us
  matrix products: 85.7 us -> 0 us
  local copies, waits for them, and re-layouts: 80.7 us -> 11.8 us
  other arithmetic: 82.6 us -> 15 us
  blocking collectives: 0 us -> 10.6 us
    pallas_call x0 -> x1, Pallas kernels: none -> 97.9 us  [one_patch(): pl.pallas_call(functools.partial(kernel, nf, nd, c, scale), out_shape=(sh...]
    unnamed x6 -> x2, waiting for transfers between devices: 97.5 us -> 0.03 us
    dot_general x6 -> x0, matrix products: 85.7 us -> none  [the longest x2 39.3 us: forward_conv(): jnp.einsum('toi,isc->tosc', weight, inputs, preferred_element_type=jnp.fl...]
    psum x1 -> x0, waiting for transfers between devices: 84.2 us -> none  [shards(): first_sum, second_sum = lax.psum((first_part, second_part), 'dp')]
    squeeze x4 -> x1, local copies, waits for them, and re-layouts: 57.2 us -> 1.86 us  [shards(): got[1]]
    unnamed x52 -> x0, other arithmetic: 40.1 us -> none
    all_gather x2 -> x1, waiting for transfers between devices: 20.1 us -> 42.7 us  [shards(): back = lax.all_gather(jnp.stack([out, igrad]), 'dp', axis=0, tiled=False)]
    mul x4 -> x0, other arithmetic: 21.9 us -> none  [the longest x1 16.4 us: shards(): output_maps = result * live[None, :, None].astype(jnp.float32)]
  transfers between devices with their start and end apart: 5 -> 2, of which waited for: 5 -> 2; matrix products, arithmetic and copies ran while one was open for 39% -> 3% of each run, Pallas kernels for 0% -> 0%
where the time goes in v1:
time: 240 us
  Pallas kernels  97.9 us (41%)
  waiting for transfers between devices  87.6 us (36%)
  between operations  16.7 us (7%)
  other arithmetic  15 us (6%)
  local copies, waits for them, and re-layouts  11.8 us (5%)
  blocking collectives  10.6 us (4%)
    pallas_call x1, Pallas kernels, one_patch(): pl.pallas_call(functools.partial(kernel, nf, nd, c, scale), out_shape=(sh...  97.9 us
    reduce_scatter x1, waiting for transfers between devices, shards(): got = lax.psum_scatter(placed, 'dp', scatter_dimension=0, tiled=False)  44.8 us
    all_gather x1, waiting for transfers between devices, shards(): back = lax.all_gather(jnp.stack([out, igrad]), 'dp', axis=0, tiled=False)  42.7 us
    unnamed x1, blocking collectives  10.6 us
  transfers between devices with their start and end apart: 2, of which 2 were waited for; matrix products, arithmetic and copies ran while one was open for 3% of the time, Pallas kernels for 0%

profile of v1, /device:TPU:0, one launch (start us, length us, event | category | flops | bytes accessed | tf_op | source)
XLA Modules:
  0.0 239.6 jit_solution(5687337976710610834)
XLA Ops:
  7.2 0.0 reduce-scatter.2.cloned.1.call-start
  7.9 1.2 dynamic-slice.6
  9.1 0.8 dynamic-update-slice
  9.9 10.6 %all-reduce = s32[8]{0:T(128)S(1)} all-reduce(s32[8]{0:T(128)S(1)} %dynamic-update-slice), channel_id=1, replica_groups=mesh['dp'=8,'filter'=4] {'dp'}, use_global_device_ids=true, to_apply=%add | all-reduce | flops 8 | bytes 64
  20.5 0.6 fusion.6
  21.1 0.6 iota_add_fusion
  21.8 0.1 fusion.5
  21.9 1.5 fusion.3
  23.4 2.6 %select_select_fusion = bf16[8,2,64,2048]{3,2,1,0:T(8,128)(2,1)} fusion(pred[8]{0:T(512)(128)(4,1)S(1)} %get-tuple-element.32, pred[8]{0:T(512)(128)(4,1)S(1)} %get-tuple-element.33, pred[8]{0:T(512)(128)(4,1)S(1)} %get-tuple-element.31, bf16[2,64,2048]{2,1,0:T(8,128)(2,1)S(1)} %get-tuple-element.21, bf16[2,64,2048]{2,1,0:T(8,128)(2,1)S(1)} %get-tuple-element.22, ...), kind=kLoop, calls=%fused_computation | loop fusion | flops 6291456 | bytes 5767192 | tf_op jit(solution)/shard_map/jit(_where)/select_n | solution.py:372
  26.0 0.0 copy-start
  26.0 0.0 copy-start.1
  26.0 0.0 reduce-scatter.2.cloned.1.call-update
  26.0 0.0 all-gather.3.cloned.1.call-start
  26.1 1.1 copy-done
  27.1 1.4 copy.15
  28.5 0.0 copy-done.1
  28.5 1.4 copy.16
  29.9 44.8 %reduce-scatter.2.cloned.1.call-done = bf16[1,2,64,2048]{3,2,1,0:T(8,128)(2,1)} async-done(((bf16[8,2,64,2048]{3,2,1,0:T(8,128)(2,1)}), bf16[1,2,64,2048]{3,2,1,0:T(8,128)(2,1)}) %reduce-scatter.2.cloned.1.call-update) | async-done | bytes 524304 | tf_op jit(solution)/shard_map/reduce_scatter | solution.py:373
  74.7 1.9 slice_bitcast_fusion
  76.6 97.9 %shard_map.84 = (bf16[64,2048]{1,0:T(8,128)(2,1)}, bf16[64,2048]{1,0:T(8,128)(2,1)}, bf16[1792,256]{1,0:T(8,128)(2,1)}, bf16[1792,256]{1,0:T(8,128)(2,1)}) custom-call(bf16[64,2048]{1,0:T(8,128)(2,1)} %get-tuple-element.24.x, bf16[64,2048]{1,0:T(8,128)(2,1)} %get-tuple-element.23.u, bf16[1728,256]{1,0:T(8,128)(2,1)} %bitcast.55, bf16[1728,256]{1,0:T(8,128)(2,1)} %bitcast.57, ...), custom_call_target="tpu_custom_call" | custom-call | flops 10871635968 | bytes 16777216 | tf_op jit(solution)/shard_map/pallas_call | solution.py:321
  174.4 0.0 copy-start.3
  174.4 2.0 pad_maximum_fusion.3
  176.4 0.0 all-gather.3.cloned.1.call-update
  176.4 0.6 fusion.9
  179.0 0.7 fusion.8
  179.6 0.0 copy-done.3
  179.6 0.0 copy-start.2
  179.6 0.1 slice.82
  179.7 1.4 convert.2
  181.1 0.0 copy-done.2
  181.1 0.1 slice.83
  181.2 1.4 convert.3
  182.6 42.7 %all-gather.3.cloned.1.call-done = bf16[16,64,2048]{2,1,0:T(8,128)(2,1)} async-done(((bf16[2,64,2048]{2,1,0:T(8,128)(2,1)}), bf16[16,64,2048]{2,1,0:T(8,128)(2,1)}) %all-gather.3.cloned.1.call-update) | async-done | bytes 4194320 | tf_op jit(solution)/shard_map/all_gather | solution.py:375
  225.3 2.7 %fusion.7 = (bf16[8,1,64,2048]{3,2,1,0:T(8,128)(2,1)S(1)}, bf16[8,1,64,2048]{3,2,1,0:T(8,128)(2,1)S(1)}) fusion(bf16[8,2,64,2048]{3,2,1,0:T(8,128)(2,1)} %bitcast.50), kind=kLoop, calls=%fused_computation.31 | loop fusion | bytes 8388608 | tf_op jit(solution)/shard_map/slice | solution.py:381
  228.0 2.2 select_bitcast_fusion.2
  230.3 1.3 pad_maximum_fusion.1
  231.5 1.2 pad_maximum_fusion
  (3 shorter events, 0.0 us)
Async XLA Ops:
  7.2 67.5 %reduce-scatter.2.cloned.1.call-start = ((), (), s32[]{:S(2)}) async-start(), calls=%async_computation.1 | async-start | bytes 4718592 | tf_op jit(solution)/shard_map/reduce_scatter | solution.py:373
  26.0 1.2 copy-start
  26.0 2.5 %copy-start.1 = (bf16[27,64,256]{2,1,0:T(8,128)(2,1)S(1)}, bf16[27,64,256]{2,1,0:T(8,128)(2,1)}, u32[]{:S(2)}) copy-start(bf16[27,64,256]{2,1,0:T(8,128)(2,1)} %param.8) | copy-start | bytes 2654212
  26.0 199.3 %all-gather.3.cloned.1.call-start = ((), (), s32[]{:S(2)}) async-start(), calls=%async_computation.2 | async-start | bytes 4718592 | tf_op jit(solution)/shard_map/all_gather | solution.py:375
  174.4 5.2 %copy-start.3 = (bf16[1792,256]{1,0:T(8,128)(2,1)S(1)}, bf16[1792,256]{1,0:T(8,128)(2,1)}, u32[]{:S(2)}) copy-start(bf16[1792,256]{1,0:T(8,128)(2,1)} %get-tuple-element.10) | copy-start | bytes 2752516
  179.6 1.5 copy-start.2
Sparse Core Ops, SparseCore 0:
  26.1 48.5 reduce-scatter.1
  176.5 48.7 all-gather.2

commit v2 on v1

v2 whole, which is shorter than its diff:
```python
import functools
import math

import jax
import jax.numpy as jnp
from jax import lax
from jax.experimental import pallas as pl
from jax.experimental.pallas import tpu as pltpu
from jax.sharding import PartitionSpec as P

CAP = 3
CELLS = 2048
PLANE = 256
PLANES = 8
SIDE = 16
MESH = pl.DeviceIdType.MESH
F32 = jnp.float32
BF16 = jnp.bfloat16

PAIRS = [(oy, oz) for oy in (-1, 0, 1) for oz in (-1, 0, 1)]


def inside(oy, oz):
    cell = lax.broadcasted_iota(jnp.int32, (1, PLANE), 1)
    y = cell // SIDE + oy
    z = cell % SIDE + oz
    return (y >= 0) & (y < SIDE) & (z >= 0) & (z < SIDE)


def moved(value, oy, oz):
    step = oy * SIDE + oz
    if step == 0:
        return value
    rolled = pltpu.roll(value, (-step) % PLANE, 1)
    return jnp.where(inside(oy, oz), rolled, jnp.zeros_like(rolled))


def remote(src, dst, send, recv, target):
    return pltpu.make_async_remote_copy(
        src_ref=src, dst_ref=dst, send_sem=send, recv_sem=recv, device_id=target, device_id_type=MESH
    )


def build_stack(c, value, stack):
    zero = jnp.zeros((9 * c, PLANE), BF16)
    stack[:, 0:PLANE] = zero
    stack[:, (PLANES + 1) * PLANE :] = zero

    def plane(p, _):
        part = value[:, pl.ds(pl.multiple_of(p * PLANE, PLANE), PLANE)].astype(F32)
        here = pl.ds(pl.multiple_of((p + 1) * PLANE, PLANE), PLANE)
        for j, (oy, oz) in enumerate(PAIRS):
            stack[j * c : (j + 1) * c, here] = moved(part, -oy, -oz).astype(BF16)
        return 0

    lax.fori_loop(0, PLANES, plane, 0)


def forward(c, value, weight, proj, finish):
    rows = 27 * c
    proj[3, 0 : 9 * c, :] = jnp.zeros((9 * c, PLANE), F32)

    def multiply(p):
        part = value[:, pl.ds(pl.multiple_of(p * PLANE, PLANE), PLANE)]
        proj[lax.rem(p, 4)] = jnp.dot(weight[...], part, preferred_element_type=F32)

    def combine(q):
        total = jnp.zeros((c, PLANE), F32)
        for j, (oy, oz) in enumerate(PAIRS):
            terms = [
                proj[lax.rem(q + 4 + ox, 4), (9 * (ox + 1) + j) * c : (9 * (ox + 1) + j + 1) * c, :]
                for ox in (-1, 0, 1)
            ]
            total = total + moved(terms[0] + terms[1] + terms[2], oy, oz)
        finish(q, total)

    def both(p, _):
        multiply(p)
        combine(p - 2)
        return 0

    multiply(jnp.int32(0))
    multiply(jnp.int32(1))
    lax.fori_loop(2, PLANES, both, 0)
    proj[0, 18 * c : rows, :] = jnp.zeros((9 * c, PLANE), F32)

    def last(q, _):
        combine(q)
        return 0

    lax.fori_loop(PLANES - 2, PLANES, last, 0)


def backward(weight_t, stack, out):
    def plane(q, _):
        part = jnp.concatenate(
            [stack[:, pl.ds(pl.multiple_of((q + 1 - ox) * PLANE, PLANE), PLANE)] for ox in (-1, 0, 1)], axis=0
        )
        value = jnp.dot(weight_t[...], part, preferred_element_type=F32)
        out[:, pl.ds(pl.multiple_of(q * PLANE, PLANE), PLANE)] = value.astype(out.dtype)
        return 0

    lax.fori_loop(0, PLANES, plane, 0)


def weight_grad(c, stack, value, out):
    for part in range(3):
        rows = pl.ds(part * 9 * c, 9 * c)
        out[rows, :] = lax.dot_general(
            stack[:, (2 - part) * PLANE : (2 - part + PLANES) * PLANE],
            value[...],
            (((1,), (1,)), ((), ())),
            preferred_element_type=F32,
        )
    rest = out.shape[0] - 27 * c
    if rest:
        out[27 * c :, :] = jnp.zeros((rest, out.shape[1]), F32)


def cap_right(n, e):
    return jnp.minimum(2 * e, n - e)


def cap_left(n, e):
    return jnp.minimum(2 * (n - e), e)


def most(n):
    return max(min(2 * e, n - e) for e in range(n + 1))


def kernel(
    nf, nd, c, scale,
    cnt, x3, u3, w1, w2, w1t, w2t,
    out, igrad, g1, g2,
    xg, hg, stack, dstack, proj, hpart, hrecv, ipart, irecv, acc1, acc2, half1, half2,
    snd1, snd2, rcv1, rcv2, counts, pre_r, pre_l, got_r, got_l, res, ret_r0, ret_r1, ret_l0, ret_l1,
    fs, fr, cs, cr, zs, zr, ns, nr, rs, rr, ls, lr, brs, brr, bls, blr,
):
    ret_r, ret_l = (ret_r0, ret_r1), (ret_l0, ret_l1)
    x, u, first = irecv.at[0], res.at[0], hrecv.at[0]
    f = lax.axis_index("filter")
    d = lax.axis_index("dp")
    nz = nd // 2
    core = lax.rem(d, 2)
    z = d // 2
    mate = d + 1 - 2 * core
    deep = most(nd)

    def fpeer(k):
        return lax.rem(f + k, nf)

    def ffrom(k):
        return lax.rem(f + nf - k, nf)

    def zpeer(k):
        return lax.rem(z + k, nz)

    def zfrom(k):
        return lax.rem(z + nz - k, nz)

    barrier = pltpu.get_barrier_semaphore()
    for k in range(1, nf):
        pl.semaphore_signal(barrier, inc=1, device_id={"filter": fpeer(k)}, device_id_type=MESH)
    for k in range(1, nd):
        pl.semaphore_signal(barrier, inc=1, device_id={"dp": lax.rem(d + k, nd)}, device_id_type=MESH)
    pl.semaphore_wait(barrier, nf + nd - 2)

    ncopies = [
        remote(cnt, counts.at[d], ns.at[k], nr.at[k], {"dp": lax.rem(d + k, nd)}) for k in range(1, nd)
    ]
    for copy in ncopies:
        copy.start()
    counts[d] = cnt[...]
    for k in range(1, nd):
        remote(
            cnt, counts.at[lax.rem(d + nd - k, nd)], ns.at[k], nr.at[k], {"dp": lax.rem(d + k, nd)}
        ).wait_recv()
    before = jnp.zeros((8, 128), jnp.int32)
    for g in range(nd):
        before = before + counts[g] * (g < d).astype(jnp.int32)
    held = cnt[...][0, 0]
    begin = before[0, 0]
    end = begin + held
    right = jnp.minimum(d + 1, nd - 1)
    left = jnp.maximum(d - 1, 0)

    def stream_r(src, dst, sems, k):
        return remote(src, dst, sems[0].at[k], sems[1].at[k], {"dp": right})

    def stream_l(src, dst, sems, k):
        return remote(src, dst, sems[0].at[k], sems[1].at[k], {"dp": left})

    def balance(n, own3, mine):
        def own(p):
            return own3[jnp.clip(p - begin, 0, CAP - 1)]

        def step(tau, _):
            kr = tau - 2 * d
            kl = tau - 2 * (nd - 1 - d)

            @pl.when((kr >= 0) & (kr < cap_right(nd, d + 1)))
            def _():
                take = kr + 1 < cap_right(nd, d)

                @pl.when(take)
                def _():
                    stream_r(pre_r.at[kr + 1], got_r.at[n, kr + 1], (rs.at[n], rr.at[n]), kr + 1).wait_recv()

                if n:
                    stream_r(pre_r.at[kr], got_r.at[0, kr], (rs.at[0], rr.at[0]), kr).wait_send()
                pre_r[kr] = own(d + 1 + kr)

                @pl.when(take)
                def _():
                    pre_r[kr] = jnp.where(d + 1 + kr < begin, got_r[n, kr + 1], pre_r[kr])

                stream_r(pre_r.at[kr], got_r.at[n, kr], (rs.at[n], rr.at[n]), kr).start()

            @pl.when((kl >= 0) & (kl < cap_left(nd, d)))
            def _():
                take = kl + 1 < cap_left(nd, d + 1)

                @pl.when(take)
                def _():
                    stream_l(pre_l.at[kl + 1], got_l.at[n, kl + 1], (ls.at[n], lr.at[n]), kl + 1).wait_recv()

                if n:
                    stream_l(pre_l.at[kl], got_l.at[0, kl], (ls.at[0], lr.at[0]), kl).wait_send()
                pre_l[kl] = own(d - 1 - kl)

                @pl.when(take)
                def _():
                    pre_l[kl] = jnp.where(d - 1 - kl >= end, got_l[n, kl + 1], pre_l[kl])

                stream_l(pre_l.at[kl], got_l.at[n, kl], (ls.at[n], lr.at[n]), kl).start()

            return 0

        lax.fori_loop(0, 2 * (nd - 1) + deep, step, 0)
        mine[...] = own(d)

        @pl.when(cap_right(nd, d) > 0)
        def _():
            stream_r(pre_r.at[0], got_r.at[n, 0], (rs.at[n], rr.at[n]), 0).wait_recv()
            mine[...] = jnp.where(d < begin, got_r[n, 0], mine[...])

        @pl.when(cap_left(nd, d + 1) > 0)
        def _():
            stream_l(pre_l.at[0], got_l.at[n, 0], (ls.at[n], lr.at[n]), 0).wait_recv()
            mine[...] = jnp.where(d >= end, got_l[n, 0], mine[...])

    def drain_balance(n):
        for k in range(deep):

            @pl.when(k < cap_right(nd, d + 1))
            def _():
                stream_r(pre_r.at[k], got_r.at[n, k], (rs.at[n], rr.at[n]), k).wait_send()

            @pl.when(k < cap_left(nd, d))
            def _():
                stream_l(pre_l.at[k], got_l.at[n, k], (ls.at[n], lr.at[n]), k).wait_send()

    def back_l(n, k):
        src = res.at[n] if k == 0 else ret_l[n].at[k - 1]
        return stream_l(src, ret_l[n].at[k], (bls.at[n], blr.at[n]), k)

    def back_r(n, k):
        src = res.at[n] if k == 0 else ret_r[n].at[k - 1]
        return stream_r(src, ret_r[n].at[k], (brs.at[n], brr.at[n]), k)

    def send_back(n, k):
        @pl.when(k < cap_right(nd, d))
        def _():
            back_l(n, k).start()

        @pl.when(k < cap_left(nd, d + 1))
        def _():
            back_r(n, k).start()

    def receive_back(n, k):
        @pl.when(k < cap_right(nd, d + 1))
        def _():
            back_l(n, k).wait_recv()

        @pl.when(k < cap_left(nd, d))
        def _():
            back_r(n, k).wait_recv()

    def drain_back(n):
        for k in range(deep):

            @pl.when(k < cap_right(nd, d))
            def _():
                back_l(n, k).wait_send()

            @pl.when(k < cap_left(nd, d + 1))
            def _():
                back_r(n, k).wait_send()

    def collect(n, target):
        for j in range(CAP):
            p = begin + j
            value = res[n]
            value = jnp.where(p > d, ret_l[n][jnp.clip(p - d - 1, 0, deep - 1)], value)
            value = jnp.where(p < d, ret_r[n][jnp.clip(d - 1 - p, 0, deep - 1)], value)
            target[j] = jnp.where(j < held, value, jnp.zeros_like(value))

    def block(i):
        return pl.ds(pl.multiple_of(i * c, c), c)

    def gather(n, own, full):
        return [
            remote(own, full.at[block(f)], fs.at[n, k], fr.at[n, k], {"filter": fpeer(k)}) for k in range(1, nf)
        ]

    def gathered(n, own, full):
        for k in range(1, nf):
            remote(own, full.at[block(ffrom(k))], fs.at[n, k], fr.at[n, k], {"filter": fpeer(k)}).wait_recv()

    def scatter(n, part, recv):
        return [
            remote(part.at[block(fpeer(k))], recv.at[k], fs.at[n, k], fr.at[n, k], {"filter": fpeer(k)})
            for k in range(1, nf)
        ]

    half = acc1.shape[0] // 2
    chunk = half // nz

    def swap(n, acc, recv):
        return remote(
            acc.at[pl.ds(pl.multiple_of((1 - core) * half, half), half)],
            recv, cs.at[n], cr.at[n], {"dp": mate},
        )

    def spread(n, acc, recv, snd, rcv):
        mine = pl.ds(pl.multiple_of(core * half, half), half)
        acc[mine, :] = acc[mine, :] + recv[...]
        started = []
        for k in range(1, nz):
            at = pl.ds(pl.multiple_of(core * half + zpeer(k) * chunk, chunk), chunk)
            snd[k] = acc[at, :].astype(BF16)
            copy = remote(snd.at[k], rcv.at[k], zs.at[n, k], zr.at[n, k], {"dp": zpeer(k) * 2 + core})
            copy.start()
            started.append(copy)
        return started

    def settle(n, acc, started, rcv, out):
        at = pl.ds(pl.multiple_of(core * half + z * chunk, chunk), chunk)
        total = acc[at, :]
        for k in range(1, nz):
            started[k - 1].wait_recv()
            total = total + rcv[k].astype(F32)
        out[at, :] = (total * scale).astype(BF16)
        sent = []
        for k in range(1, nz):
            copy = remote(
                out.at[at], out.at[at], zs.at[n + 2, k], zr.at[n + 2, k], {"dp": zpeer(k) * 2 + core}
            )
            copy.start()
            sent.append(copy)
        return sent

    def share(n, out):
        for k in range(1, nz):
            at = pl.ds(pl.multiple_of(core * half + zfrom(k) * chunk, chunk), chunk)
            remote(
                out.at[at], out.at[at], zs.at[n + 2, k], zr.at[n + 2, k], {"dp": zpeer(k) * 2 + core}
            ).wait_recv()
        mine = pl.ds(pl.multiple_of(core * half, half), half)
        copy = remote(out.at[mine], out.at[mine], cs.at[n + 2], cr.at[n + 2], {"dp": mate})
        copy.start()
        return copy

    def shared(n, out):
        other = pl.ds(pl.multiple_of((1 - core) * half, half), half)
        remote(out.at[other], out.at[other], cs.at[n + 2], cr.at[n + 2], {"dp": mate}).wait_recv()

    balance(0, x3, x)
    copies = gather(0, x, xg)
    for copy in copies:
        copy.start()
    xg[block(f), :] = x[...]
    balance(1, u3, u)

    build_stack(c, u, stack)
    backward(w2t, stack, hpart)
    hcopies = scatter(1, hpart, hrecv)
    for copy in hcopies:
        copy.start()

    gathered(0, x, xg)

    def activate(q, total):
        at = pl.ds(pl.multiple_of(q * PLANE, PLANE), PLANE)
        first[:, at] = total
        hg[block(f), at] = (total / (1.0 + jnp.exp(-total))).astype(BF16)

    forward(c, xg, w1, proj, activate)
    own_hidden = hg.at[block(f)]
    gcopies = gather(2, own_hidden, hg)
    for copy in gcopies:
        copy.start()

    for k in range(1, nf):
        hcopies[k - 1].wait_recv()

    def deltas(q, _):
        at = pl.ds(pl.multiple_of(q * PLANE, PLANE), PLANE)
        grad = hpart[block(f), at]
        for k in range(1, nf):
            grad = grad + hrecv[k, :, at]
        a = first[:, at]
        sg = 1.0 / (1.0 + jnp.exp(-a))
        first[:, at] = grad * sg * (1.0 + a * (1.0 - sg))
        return 0

    lax.fori_loop(0, PLANES, deltas, 0)
    build_stack(c, first, dstack)
    backward(w1t, dstack, ipart)
    icopies = scatter(3, ipart, irecv)
    for copy in icopies:
        copy.start()
    weight_grad(c, dstack, xg, acc1)
    swap1 = swap(0, acc1, half1)
    swap1.start()

    gathered(2, own_hidden, hg)
    weight_grad(c, stack, hg, acc2)
    swap2 = swap(1, acc2, half2)
    swap2.start()
    swap1.wait_recv()
    spread1 = spread(0, acc1, half1, snd1, rcv1)

    def keep(q, total):
        res[0, :, pl.ds(pl.multiple_of(q * PLANE, PLANE), PLANE)] = total.astype(BF16)

    forward(c, hg, w2, proj, keep)
    send_back(0, 0)
    swap2.wait_recv()
    spread2 = spread(1, acc2, half2, snd2, rcv2)

    for k in range(1, nf):
        icopies[k - 1].wait_recv()

    def inputs(q, _):
        at = pl.ds(pl.multiple_of(q * PLANE, PLANE), PLANE)
        grad = ipart[block(f), at].astype(F32)
        for k in range(1, nf):
            grad = grad + irecv[k, :, at].astype(F32)
        res[1, :, at] = grad.astype(BF16)
        return 0

    lax.fori_loop(0, PLANES, inputs, 0)
    send_back(1, 0)
    sent1 = settle(0, acc1, spread1, rcv1, g1)
    for n in range(2):
        for k in range(deep):
            receive_back(n, k)
            if k + 1 < deep:
                send_back(n, k + 1)
        if n == 0:
            sent2 = settle(1, acc2, spread2, rcv2, g2)
            last1 = share(0, g1)
            collect(0, out)
    last2 = share(1, g2)
    collect(1, igrad)
    shared(0, g1)
    shared(1, g2)
    for copy in ncopies + copies + hcopies + gcopies + icopies + [swap1, swap2] + spread1 + spread2:
        copy.wait_send()
    for copy in sent1 + sent2 + [last1, last2]:
        copy.wait_send()
    for n in range(2):
        drain_back(n)
    drain_balance(1)


def patches_kernel(cnt, x3, u3, w1, w2, nf, nd):
    c = x3.shape[1]
    deep = most(nd)
    rows = 27 * c
    wide = w1.shape[-1]
    padded = -(-rows // (16 * nd)) * 16 * nd
    half = padded // 2
    nz = nd // 2
    chunk = half // nz
    scale = 1.0 / math.sqrt(nd * CELLS)
    w1 = w1.reshape(rows, wide)
    w2 = w2.reshape(rows, wide)
    vmem = pl.BlockSpec(memory_space=pltpu.VMEM)
    shape = jax.ShapeDtypeStruct
    flops = 12 * rows * wide * CELLS
    return pl.pallas_call(
        functools.partial(kernel, nf, nd, c, scale),
        out_shape=(
            shape((CAP, c, CELLS), BF16), shape((CAP, c, CELLS), BF16), shape((padded, wide), BF16), shape((padded, wide), BF16)
        ),
        in_specs=[vmem] * 7,
        out_specs=(vmem,) * 4,
        scratch_shapes=[
            pltpu.VMEM((wide, CELLS), BF16),
            pltpu.VMEM((wide, CELLS), BF16),
            pltpu.VMEM((9 * c, CELLS + 2 * PLANE), BF16),
            pltpu.VMEM((9 * c, CELLS + 2 * PLANE), BF16),
            pltpu.VMEM((4, rows, PLANE), F32),
            pltpu.VMEM((wide, CELLS), F32),
            pltpu.VMEM((nf, c, CELLS), F32),
            pltpu.VMEM((wide, CELLS), BF16),
            pltpu.VMEM((nf, c, CELLS), BF16),
            pltpu.VMEM((padded, wide), F32),
            pltpu.VMEM((padded, wide), F32),
            pltpu.VMEM((half, wide), F32),
            pltpu.VMEM((half, wide), F32),
            pltpu.VMEM((nz, chunk, wide), BF16),
            pltpu.VMEM((nz, chunk, wide), BF16),
            pltpu.VMEM((nz, chunk, wide), BF16),
            pltpu.VMEM((nz, chunk, wide), BF16),
            pltpu.VMEM((nd, 8, 128), jnp.int32),
            pltpu.VMEM((deep, c, CELLS), BF16),
            pltpu.VMEM((deep, c, CELLS), BF16),
            pltpu.VMEM((2, deep, c, CELLS), BF16),
            pltpu.VMEM((2, deep, c, CELLS), BF16),
            pltpu.VMEM((2, c, CELLS), BF16),
            pltpu.VMEM((deep, c, CELLS), BF16),
            pltpu.VMEM((deep, c, CELLS), BF16),
            pltpu.VMEM((deep, c, CELLS), BF16),
            pltpu.VMEM((deep, c, CELLS), BF16),
            pltpu.SemaphoreType.DMA((4, nf)),
            pltpu.SemaphoreType.DMA((4, nf)),
            pltpu.SemaphoreType.DMA((4,)),
            pltpu.SemaphoreType.DMA((4,)),
            pltpu.SemaphoreType.DMA((4, nz)),
            pltpu.SemaphoreType.DMA((4, nz)),
            pltpu.SemaphoreType.DMA((nd,)),
            pltpu.SemaphoreType.DMA((nd,)),
        ] + [pltpu.SemaphoreType.DMA((2, deep))] * 8,
        compiler_params=pltpu.CompilerParams(
            collective_id=0, has_side_effects=True, vmem_limit_bytes=58 * 1024 * 1024
        ),
        cost_estimate=pl.CostEstimate(flops=flops, bytes_accessed=16 * 1024 * 1024, transcendentals=0),
    )(cnt, x3, u3, w1, w2, w1.T, w2.T)


def shards(nf, nd, patches, cotangent, first_weight, second_weight, counts):
    c = patches.shape[0]
    cnt = jnp.broadcast_to(counts[:, None], (8, 128))
    out, igrad, g1, g2 = patches_kernel(
        cnt, jnp.swapaxes(patches, 0, 1), jnp.swapaxes(cotangent, 0, 1), first_weight, second_weight, nf, nd
    )
    rows = 27 * c
    shape = first_weight.shape
    return (
        jnp.swapaxes(out, 0, 1).astype(F32),
        jnp.swapaxes(igrad, 0, 1).astype(F32),
        g1[:rows].astype(F32).reshape(shape),
        g2[:rows].astype(F32).reshape(shape),
    )


def solution(mesh):
    placed = (
        P("filter", "dp", None),
        P("filter", "dp", None),
        P(None, "filter", None),
        P(None, "filter", None),
        P("dp"),
    )
    return jax.shard_map(
        functools.partial(shards, mesh.shape["filter"], mesh.shape["dp"]),
        mesh=mesh,
        in_specs=placed,
        out_specs=(
            P("filter", "dp", None),
            P("filter", "dp", None),
            P(None, "filter", None),
            P(None, "filter", None),
        ),
        check_vma=False,
    )
```

time: 240 us -> 211 us (0.88); the launches traced: 240 us -> 207 us
  Pallas kernels: 97.9 us -> 195 us
  waiting for transfers between devices: 87.6 us -> 0 us
  between operations: 16.7 us -> 1.32 us
  blocking collectives: 10.6 us -> 0 us
  other arithmetic: 15 us -> 6.31 us
  local copies, waits for them, and re-layouts: 11.8 us -> 4.37 us
    pallas_call x1, Pallas kernels: 97.9 us -> 195 us  [patches_kernel(): pl.pallas_call(functools.partial(kernel, nf, nd, c, scale), out_shape=(sh...]
    reduce_scatter x1 -> x0, waiting for transfers between devices: 44.8 us -> none  [shards(): got = lax.psum_scatter(placed, 'dp', scatter_dimension=0, tiled=False)]
    all_gather x1 -> x0, waiting for transfers between devices: 42.7 us -> none  [shards(): back = lax.all_gather(jnp.stack([out, igrad]), 'dp', axis=0, tiled=False)]
    unnamed x1 -> x0, blocking collectives: 10.6 us -> none
    select_n x2 -> x0, other arithmetic: 4.87 us -> none  [the longest x1 2.63 us: shards(): jnp.where(hit[:, j][:, None, None, None], pairs[None, :, :, j], placed)]
    another operation x3 -> x0, other arithmetic: 4.45 us -> none  [the longest x2 2.5 us: shards(): outs.append(jnp.stack(columns, axis=1))]
    slice x3 -> x0, local copies, waits for them, and re-layouts: 3.97 us -> none  [the longest x1 2.73 us: shards(): back[:, n]]
    convert_element_type x0 -> x1, other arithmetic: none -> 3.49 us  [shards(): jnp.swapaxes(igrad, 0, 1).astype(F32)]
  transfers between devices with their start and end apart: 2 -> 0, of which waited for: 2 -> 0; matrix products, arithmetic and copies ran while one was open for 3% -> 0% of each run, Pallas kernels for 0% -> 0%
where the time goes in v2:
time: 211 us; the launch traced here: 207 us
  Pallas kernels  195 us (92%)
  other arithmetic  6.31 us (3%)
  local copies, waits for them, and re-layouts  4.37 us (2%)
    pallas_call x1, Pallas kernels, patches_kernel(): pl.pallas_call(functools.partial(kernel, nf, nd, c, scale), out_shape=(sh...  195 us

profile of v2, /device:TPU:0, one launch (start us, length us, event | category | flops | bytes accessed | tf_op | source)
XLA Modules:
  0.0 207.1 jit_solution(5546115053430543739)
XLA Ops:
  0.6 0.0 copy-start
  0.6 2.3 %copy.13 = bf16[1728,256]{0,1:T(8,128)(2,1)} copy(bf16[1728,256]{1,0:T(8,128)(2,1)} %bitcast.20) | data formatting | bytes 1769472 | tf_op jit(solution)/shard_map/reshape | solution.py:489
  2.9 0.0 copy-done
  2.9 1.4 copy.14
  4.9 0.6 broadcast_in_dim.9.cnt
  5.5 195.1 %shard_map.84 = (bf16[3,64,2048]{2,1,0:T(8,128)(2,1)}, bf16[3,64,2048]{2,1,0:T(8,128)(2,1)}, bf16[1792,256]{1,0:T(8,128)(2,1)}, bf16[1792,256]{1,0:T(8,128)(2,1)}) custom-call(s32[8,128]{1,0:T(8,128)} %broadcast_in_dim.9.cnt, bf16[3,64,2048]{2,1,0:T(8,128)(2,1)} %bitcast.24, bf16[3,64,2048]{2,1,0:T(8,128)(2,1)} %bitcast.25, bf16[1728,256]{1,0:T(8,128)(2,1)} %bitcast.21, ...), custom_call_target="tpu_custom_call" | custom-call | flops 10871635968 | bytes 16777216 | tf_op jit(solution)/shard_map/pallas_call | solution.py:494
  200.7 0.0 copy-start.2
  200.7 3.5 %convert_bitcast_fusion = (f32[64,3,2048]{2,0,1:T(8,128)}, f32[64,3,2048]{2,0,1:T(8,128)}) fusion(bf16[3,64,2048]{2,1,0:T(8,128)(2,1)} %get-tuple-element.9, bf16[3,64,2048]{2,1,0:T(8,128)(2,1)} %get-tuple-element.8), kind=kLoop, calls=%fused_computation | loop fusion | flops 786432 | bytes 4718592 | tf_op jit(solution)/shard_map/convert_element_type | solution.py:555
  204.2 0.0 copy-done.2
  204.2 0.1 slice.6
  204.2 0.0 copy-start.1
  204.2 1.4 convert.4
  205.6 0.0 copy-done.1
  205.7 0.1 slice.7
  205.7 1.4 convert.5
Async XLA Ops:
  0.6 2.3 %copy-start = (bf16[27,64,256]{2,1,0:T(8,128)(2,1)S(1)}, bf16[27,64,256]{2,1,0:T(8,128)(2,1)}, u32[]{:S(2)}) copy-start(bf16[27,64,256]{2,1,0:T(8,128)(2,1)} %param.8) | copy-start | bytes 2654212
  200.7 3.5 %copy-start.2 = (bf16[1792,256]{1,0:T(8,128)(2,1)S(1)}, bf16[1792,256]{1,0:T(8,128)(2,1)}, u32[]{:S(2)}) copy-start(bf16[1792,256]{1,0:T(8,128)(2,1)} %get-tuple-element.10) | copy-start | bytes 2752516
  204.2 1.4 copy-start.1
